TPU v7x, 512 devices: a whole 4x4x16 slice. The times are simulated.
512 devices in a mesh: gx: 32 (over z, core), gy: 16 (over y, x).
Axes of the slice: x: 4, y: 4, z: 16, core: 2. Of those that a mesh axis runs over, the one named last changes fastest.
Arguments:
- solution: float32 [512, 65536], P(None, ('gx', 'gy')), may hold values from -6 to 6
- residual: float32 [512, 65536], P(None, ('gx', 'gy')), may hold values from -60 to 60
- metric_diag: bfloat16 [3, 512, 65536], P(None, None, ('gx', 'gy')), may hold values from 0.039794922 to 0.3984375
- metric_cross: bfloat16 [3, 512, 65536], P(None, None, ('gx', 'gy')), may hold values from -0.017944336 to 0.017944336
- fdm_vectors: float32 [3, 8, 8, 65536], P(None, None, None, ('gx', 'gy')), may hold values from -5 to 5
- fdm_values: float32 [3, 8, 65536], P(None, None, ('gx', 'gy')), may hold values from 0.05 to 20
- vertex_ids: int32 [8, 65536], P(None, ('gx', 'gy')), may hold values from 0 to 8191
- coarse_inverse: float32 [8192, 8192], P(('gx', 'gy')), may hold values from -0.2 to 0.2, as said below
- elem_live: int32 [512], P(('gx', 'gy')), may hold values from 80 to 128, as said below
- section_face: int32 [512, 16, 20], P(('gx', 'gy')), may hold values from -1 to 767, as said below
- section_code: int32 [512, 16, 20], P(('gx', 'gy')), may hold values from 0 to 7, as said below
- pipe_face: int32 [512, 2, 64], P(('gx', 'gy')), may hold values from 0 to 767, as said below
- pipe_code: int32 [512, 2, 64], P(('gx', 'gy')), may hold values from 0 to 7, as said below
Outputs:
- solution_out: float32 [512, 65536], P(None, ('gx', 'gy'))
- residual_out: float32 [512, 65536], P(None, ('gx', 'gy'))
- norm_ratio: float32 [1], replicated
Inputs may be any that keep to these rules, and one draw needn't show every extreme that they name: `elem_live`: one device holds all 128 slots in every draw. A face id 6 e + f names face f of slot e of the device, with e below the device's elem_live; no id appears twice on a device over section_face and pipe_face; -1 marks an empty slot, and in each peer's row the slots holding faces come first. Slot (q, c) of device (x, y) holds a face exactly when slot (y, c) of device (x, q) does; in the row q = y they come in pairs (c, c xor 1). Each device's rows for peers y - 1, y + 1 and y + 16 / 2 (mod 16) are full; rows for other peers more than two places away (mod 16) are empty. `section_code`: with inv(o) = o for o < 4 and 4 + 2 (o mod 2) + floor((o mod 4) / 2) for o >= 4, the codes of two paired slots are inv of each other; empty slots hold 0. `pipe_face`: every slot holds a face, as for section_face. `pipe_code`: the codes of two paired slots are inv of each other, as for section_code. `coarse_inverse`: Symmetric.
All inputs are finite; a program needn't handle non-finite values.
Results may differ from a plain program's by a relative error of at most 0.0003.
Values sent between devices are 32-bit elements; how exact they have to be, the bound alone decides.
A program may use at most 64 MiB of HBM per device.

v0:
```python
import jax
import jax.numpy as jnp
from jax import lax
from jax.sharding import PartitionSpec as P

EDGE = 8
top_precision = lax.Precision.HIGHEST


def padded(block, sides, width):
    for axis, dim in sides:
        count = lax.axis_size(axis)
        forward = [(i, i + 1) for i in range(count - 1)]
        forward.append((count - 1, 0))
        backward = [(target, source) for source, target in forward]
        low = lax.ppermute(
            lax.slice_in_dim(block, block.shape[dim] - width, None, axis=dim), axis, forward
        )
        high = lax.ppermute(lax.slice_in_dim(block, 0, width, axis=dim), axis, backward)
        block = jnp.concatenate([low, block, high], axis=dim)
    return block


def node_points():
    node_index = jnp.arange(EDGE).astype(jnp.float32)
    return -jnp.cos(jnp.pi * node_index / (EDGE - 1))


def derivative_matrix():
    points = node_points()
    node_index = jnp.arange(EDGE)
    weights = jnp.where((node_index == 0) | (node_index == EDGE - 1), 2.0, 1.0).astype(jnp.float32)
    parity = jnp.where((node_index[:, None] + node_index[None, :]) % 2 == 0, 1.0, -1.0).astype(
        jnp.float32
    )
    identity = jnp.eye(EDGE, dtype=jnp.float32)
    spacing = points[:, None] - points[None, :] + identity
    offdiag = weights[:, None] / weights[None, :] * parity / spacing * (1.0 - identity)
    return offdiag - jnp.diag(jnp.sum(offdiag, axis=1))


def corner_table():
    points = node_points()
    hat_values = jnp.stack([(1.0 - points) * 0.5, (1.0 + points) * 0.5])
    corner_weights = (
        hat_values[:, None, None, :, None, None]
        * hat_values[None, :, None, None, :, None]
        * hat_values[None, None, :, None, None, :]
    )
    return corner_weights.reshape(8, EDGE**3)


def contract(matrices, element_cube, axis):
    moved = jnp.moveaxis(element_cube, axis, 0)
    total = matrices[0][:, None, None, :] * moved[0][None]
    for index in range(1, EDGE):
        total = total + matrices[index][:, None, None, :] * moved[index][None]
    return jnp.moveaxis(total, 0, axis)


def orient_columns(face_cols, orient_codes):
    face_grid = face_cols.reshape(EDGE, EDGE, -1)
    face_grid = jnp.where((orient_codes % 2 == 1)[None, None, :], face_grid[::-1, :, :], face_grid)
    face_grid = jnp.where(
        (orient_codes // 2 % 2 == 1)[None, None, :], face_grid[:, ::-1, :], face_grid
    )
    face_grid = jnp.where(
        (orient_codes >= 4)[None, None, :], jnp.swapaxes(face_grid, 0, 1), face_grid
    )
    return face_grid.reshape(EDGE * EDGE, -1)


def fdm_solve(element_cube, vectors, values):
    spectral = contract(vectors[0], element_cube, 0)
    spectral = contract(vectors[1], spectral, 1)
    spectral = contract(vectors[2], spectral, 2)
    eigen_sums = (
        values[0][:, None, None, :] + values[1][None, :, None, :] + values[2][None, None, :, :]
    )
    spectral = spectral / eigen_sums
    restored = contract(jnp.swapaxes(vectors[0], 0, 1), spectral, 0)
    restored = contract(jnp.swapaxes(vectors[1], 0, 1), restored, 1)
    return contract(jnp.swapaxes(vectors[2], 0, 1), restored, 2)


def local_operator(field, diag_part, cross_part, derivative):
    element_cube = field.reshape(EDGE, EDGE, EDGE, -1)
    diagonal = diag_part.astype(jnp.float32).reshape(3, EDGE, EDGE, EDGE, -1)
    cross_terms = cross_part.astype(jnp.float32).reshape(3, EDGE, EDGE, EDGE, -1)
    forward = jnp.transpose(derivative)[:, :, None]
    backward = derivative[:, :, None]
    grad_first = contract(forward, element_cube, 0)
    grad_second = contract(forward, element_cube, 1)
    grad_third = contract(forward, element_cube, 2)
    flux_first = (
        diagonal[0] * grad_first + cross_terms[0] * grad_second + cross_terms[1] * grad_third
    )
    flux_second = (
        cross_terms[0] * grad_first + diagonal[1] * grad_second + cross_terms[2] * grad_third
    )
    flux_third = (
        cross_terms[1] * grad_first + cross_terms[2] * grad_second + diagonal[2] * grad_third
    )
    curvature = jnp.sum(
        grad_first * flux_first + grad_second * flux_second + grad_third * flux_third
    ) + jnp.sum(element_cube * element_cube)
    applied = contract(backward, flux_first, 0)
    applied = applied + contract(backward, flux_second, 1)
    applied = applied + contract(backward, flux_third, 2)
    return ((applied + element_cube).reshape(EDGE**3, -1), curvature)


def face_sum(field, section_face, section_code, pipe_face, pipe_code):
    element_cube = field.reshape(EDGE, EDGE, EDGE, -1)
    slot_count = element_cube.shape[3]
    stacked = jnp.stack(
        [
            element_cube[0],
            element_cube[EDGE - 1],
            element_cube[:, 0],
            element_cube[:, EDGE - 1],
            element_cube[:, :, 0],
            element_cube[:, :, EDGE - 1],
        ],
        axis=-1,
    )
    face_values = stacked.reshape(EDGE * EDGE, slot_count * 6)
    face_count = face_values.shape[1]
    peer_count = section_face.shape[1]
    capacity = section_face.shape[2]
    wanted = section_face[0].reshape(-1)
    picked = jnp.take(face_values, jnp.maximum(wanted, 0), axis=1)
    outgoing = jnp.where((wanted >= 0)[None, :], picked, 0.0).reshape(
        EDGE * EDGE, peer_count, capacity
    )
    own_index = lax.axis_index("gy")
    arrived = lax.all_to_all(outgoing, "gy", split_axis=1, concat_axis=1, tiled=True)
    swapped = arrived.reshape(EDGE * EDGE, peer_count, capacity // 2, 2)[..., ::-1].reshape(
        EDGE * EDGE, peer_count, capacity
    )
    arrived = jnp.where((jnp.arange(peer_count) == own_index)[None, :, None], swapped, arrived)
    incoming = orient_columns(
        arrived.reshape(EDGE * EDGE, peer_count * capacity), section_code[0].reshape(-1)
    )
    pipe_ids = pipe_face[0]
    pipe_width = pipe_ids.shape[1]
    boundary = jnp.take(face_values, pipe_ids.reshape(-1), axis=1).reshape(
        EDGE * EDGE, 2, pipe_width
    )
    extended = padded(boundary, (("gx", 1),), 1)
    beside = jnp.concatenate([extended[:, 0], extended[:, 3]], axis=1)
    beside = orient_columns(beside, pipe_code[0].reshape(-1))
    targets = jnp.concatenate([wanted, pipe_ids.reshape(-1)])
    placed = jnp.where(targets < 0, face_count, targets)
    face_extra = (
        jnp.zeros((EDGE * EDGE, face_count), jnp.float32)
        .at[:, placed]
        .add(jnp.concatenate([incoming, beside], axis=1), mode="drop")
    )
    face_parts = face_extra.reshape(EDGE, EDGE, slot_count, 6)
    element_cube = element_cube.at[0].add(face_parts[..., 0])
    element_cube = element_cube.at[EDGE - 1].add(face_parts[..., 1])
    element_cube = element_cube.at[:, 0].add(face_parts[..., 2])
    element_cube = element_cube.at[:, EDGE - 1].add(face_parts[..., 3])
    element_cube = element_cube.at[:, :, 0].add(face_parts[..., 4])
    element_cube = element_cube.at[:, :, EDGE - 1].add(face_parts[..., 5])
    return element_cube.reshape(EDGE**3, -1)


def on_device(
    solution,
    residual,
    metric_diag,
    metric_cross,
    fdm_vectors,
    fdm_values,
    vertex_ids,
    coarse_inverse,
    elem_live,
    section_face,
    section_code,
    pipe_face,
    pipe_code,
):
    slot_count = residual.shape[1]
    alive_mask = (jnp.arange(slot_count) < elem_live[0]).astype(jnp.float32)
    rmask = residual * alive_mask[None, :]
    corner_weights = corner_table()
    derivative = derivative_matrix()
    corners = jnp.dot(corner_weights, rmask, precision=top_precision)
    coarse_partial = jax.ops.segment_sum(
        corners.reshape(-1), vertex_ids.reshape(-1), num_segments=coarse_inverse.shape[1]
    )
    coarse_rhs = lax.psum(coarse_partial, ("gx", "gy"))
    own_values = jnp.dot(coarse_inverse, coarse_rhs, precision=top_precision)
    coarse_sol = lax.all_gather(own_values, ("gx", "gy"), axis=0, tiled=True)
    smooth = fdm_solve(rmask.reshape(EDGE, EDGE, EDGE, -1), fdm_vectors, fdm_values).reshape(
        EDGE**3, -1
    )
    summed = face_sum(smooth, section_face, section_code, pipe_face, pipe_code)
    lifted = jnp.dot(corner_weights.T, coarse_sol[vertex_ids], precision=top_precision)
    direction = alive_mask[None, :] * (summed + lifted)
    applied, curvature_local = local_operator(direction, metric_diag, metric_cross, derivative)
    image = face_sum(applied, section_face, section_code, pipe_face, pipe_code)
    precond_local = jnp.sum(rmask * direction)
    norm_local = jnp.sum(rmask * rmask)
    precond_dot, curvature, old_norm = lax.psum(
        (precond_local, curvature_local, norm_local), ("gx", "gy")
    )
    step_length = precond_dot / curvature
    residual_out = rmask - step_length * image
    fresh_norm = lax.psum(jnp.sum(residual_out * residual_out), ("gx", "gy"))
    solution_out = alive_mask[None, :] * (solution + step_length * direction)
    norm_ratio = (fresh_norm / old_norm).reshape(1)
    return (solution_out, residual_out, norm_ratio)


def solution(mesh):
    placed = (
        P(None, ("gx", "gy")),
        P(None, ("gx", "gy")),
        P(None, None, ("gx", "gy")),
        P(None, None, ("gx", "gy")),
        P(None, None, None, ("gx", "gy")),
        P(None, None, ("gx", "gy")),
        P(None, ("gx", "gy")),
        P(("gx", "gy"), None),
        P(("gx", "gy")),
        P(("gx", "gy"), None, None),
        P(("gx", "gy"), None, None),
        P(("gx", "gy"), None, None),
        P(("gx", "gy"), None, None),
    )
    return jax.shard_map(
        on_device,
        mesh=mesh,
        in_specs=placed,
        out_specs=(P(None, ("gx", "gy")), P(None, ("gx", "gy")), P()),
        check_vma=False,
    )
```

profile of v0, /device:TPU:1, one launch (start us, length us, event | category | flops | bytes accessed | tf_op | source)
XLA Modules:
  0.0 567.3 jit_solution(12377010773833954774)
XLA Ops:
  6.8 2.3 copy.389
  9.0 2.5 reshape.1869
  14.6 7.6 %all-to-all-start = ((f32[16,1,1280]{2,1,0:T(1,128)}), f32[16,1,1280]{2,1,0:T(1,128)}, u32[]{:S(2)}, u32[]{:S(2)}) async-start(f32[16,1,1280]{2,1,0:T(1,128)} %reshape.1990), calls=%async_computation | async-start | bytes 163840 | tf_op jit(solution)/shard_map/all_to_all | solution.py:137
  23.7 2.5 collective-permute-start
  30.1 5.9 %scatter_custom_fusion.1 = f32[8192]{0:T(1024)S(1)} fusion(s32[1024]{0:T(1024)S(1)} %bitcast.649, f32[1024]{0:T(1024)S(1)} %convolution_bitcast_fusion, f32[]{:T(128)} %constant.402.clone.1), kind=kCustom, calls=%fused_computation.199 | custom fusion | flops 1024 | bytes 32772 | tf_op jit(solution)/shard_map/scatter-add | solution.py:191
  36.1 108.5 %psum.35 = f32[8192]{0:T(1024)S(1)} all-reduce(f32[8192]{0:T(1024)S(1)} %scatter_custom_fusion.1), channel_id=1, replica_groups=mesh['gx'=32,'gy'=16] {'gx','gy'}, use_global_device_ids=true, to_apply=%region_2.5 | all-reduce | flops 8192 | bytes 65536 | tf_op jit(solution)/shard_map/psum | solution.py:194
  169.9 99.5 %all-reduce = f32[8192]{0:T(1024)S(1)} all-reduce(f32[8192]{0:T(1024)S(1)} %dynamic-update-slice.36), channel_id=1, replica_groups=mesh['gx'=32,'gy'=16] {'gx','gy'}, use_global_device_ids=true, to_apply=%add | all-reduce | flops 8192 | bytes 65536
  269.4 10.5 %gather_fusion = f32[1024]{0:T(1024)} fusion(f32[8192]{0:T(1024)S(1)} %all-reduce, s32[1024]{0:T(1024)S(1)} %fusion.40), kind=kCustom, calls=%fused_computation.4 | custom fusion | bytes 12288 | tf_op jit(solution)/shard_map/gather | solution.py:201
  283.5 2.3 scatter_custom_fusion
  285.7 2.6 reshape.1876
  288.4 3.4 fusion.54
  291.8 1.9 copy.456
  301.8 2.0 multiply_reduce_fusion
  309.7 2.3 copy.428
  312.0 2.4 reshape.1886
  317.3 4.2 all-to-all-start.1
  322.3 1.8 collective-permute-start.2
  339.6 2.9 add_reduce_fusion
  343.7 102.5 %all-reduce.2 = (f32[]{:T(128)}, f32[]{:T(128)}) all-reduce(f32[]{:T(128)} %get-tuple-element.150, f32[]{:T(128)S(6)} %add.970), channel_id=1, replica_groups=mesh['gx'=32,'gy'=16] {'gx','gy'}, use_global_device_ids=true, to_apply=%region_4.7 | all-reduce | flops 2 | bytes 16 | tf_op jit(solution)/shard_map/psum | solution.py:207
  447.6 1.7 add_multiply_fusion
  453.1 2.5 scatter_custom_fusion.2
  455.7 2.6 reshape.1893
  458.3 2.9 fusion.53
  465.4 99.4 %all-reduce.1 = (f32[]{:T(128)}, f32[]{:T(128)}) all-reduce(f32[]{:T(128)} %get-tuple-element.156, f32[]{:T(128)} %get-tuple-element.149), channel_id=1, replica_groups=mesh['gx'=32,'gy'=16] {'gx','gy'}, use_global_device_ids=true, to_apply=%region_11.14 | all-reduce | flops 2 | bytes 16 | tf_op jit(solution)/shard_map/psum | solution.py:212
  (523 shorter events, 81.5 us)
Async XLA Ops:
  0.6 147.6 %copy-start = (f32[16,8192]{1,0:T(8,128)S(1)}, f32[16,8192]{1,0:T(8,128)}, u32[]{:S(2)}) copy-start(f32[16,8192]{1,0:T(8,128)} %param.48) | copy-start | bytes 1572868
  9.0 135.9 %copy-start.2 = (bf16[3,512,128]{2,1,0:T(8,128)(2,1)S(1)}, bf16[3,512,128]{2,1,0:T(8,128)(2,1)}, u32[]{:S(2)}) copy-start(bf16[3,512,128]{2,1,0:T(8,128)(2,1)} %param.44) | copy-start | bytes 1179652
  11.5 134.5 %copy-start.1 = (bf16[3,512,128]{2,1,0:T(8,128)(2,1)S(1)}, bf16[3,512,128]{2,1,0:T(8,128)(2,1)}, u32[]{:S(2)}) copy-start(bf16[3,512,128]{2,1,0:T(8,128)(2,1)} %param.43) | copy-start | bytes 1179652
  12.5 134.4 %copy-start.110 = (s32[1024]{0:T(1024)}, s32[1024]{0:T(1024)S(1)}, u32[]{:S(2)}) copy-start(s32[1024]{0:T(1024)S(1)} %get-tuple-element.373) | copy-start | bytes 12292
  14.6 265.5 %all-to-all-start = ((f32[16,1,1280]{2,1,0:T(1,128)}), f32[16,1,1280]{2,1,0:T(1,128)}, u32[]{:S(2)}, u32[]{:S(2)}) async-start(f32[16,1,1280]{2,1,0:T(1,128)} %reshape.1990), calls=%async_computation | async-start | bytes 163840 | tf_op jit(solution)/shard_map/all_to_all | solution.py:137
  23.5 256.5 %copy-start.66 = (pred[128]{0:T(512)(128)(4,1)}, pred[128]{0:T(512)(128)(4,1)S(1)}, u32[]{:S(2)}) copy-start(pred[128]{0:T(512)(128)(4,1)S(1)} %get-tuple-element.360) | copy-start | bytes 388
  23.7 256.2 %collective-permute-start = (f32[64,1,64]{2,0,1:T(8,128)S(1)}, f32[64,1,64]{2,0,1:T(8,128)S(1)}, u32[]{:S(2)}, u32[]{:S(2)}) collective-permute-start(f32[64,1,64]{2,0,1:T(8,128)S(1)} %copy.454), channel_id=1, source_target_pairs={{0,16},{16,32},{32,48},{48,64},{64,80},{80,96},{96,112},{112,128},... | collective-permute-start | bytes 49160 | tf_op jit(solution)/shard_map/ppermute | solution.py:16
  26.8 253.1 %collective-permute-start.1 = (f32[64,1,64]{2,0,1:T(8,128)}, f32[64,1,64]{2,0,1:T(8,128)S(1)}, u32[]{:S(2)}, u32[]{:S(2)}) collective-permute-start(f32[64,1,64]{2,0,1:T(8,128)} %copy.455), channel_id=1, source_target_pairs={{16,0},{32,16},{48,32},{64,48},{80,64},{96,80},{112,96},{128,112},... | collective-permute-start | bytes 49160 | tf_op jit(solution)/shard_map/ppermute | solution.py:19
  144.9 23.5 %copy-start.46 = (f32[8]{0:T(128)}, f32[8]{0:T(128)S(1)}, u32[]{:S(2)}) copy-start(f32[8]{0:T(128)S(1)} %get-tuple-element.348) | copy-start | bytes 100
  145.0 24.1 %copy-start.44 = (f32[8]{0:T(128)}, f32[8]{0:T(128)S(1)}, u32[]{:S(2)}) copy-start(f32[8]{0:T(128)S(1)} %get-tuple-element.347) | copy-start | bytes 100
  152.5 127.5 %copy-start.83 = (pred[128]{0:T(512)(128)(4,1)S(1)}, pred[128]{0:T(512)(128)(4,1)}, u32[]{:S(2)}) copy-start(pred[128]{0:T(512)(128)(4,1)} %get-tuple-element.361) | copy-start | bytes 388
  152.6 127.5 %copy-start.117 = (pred[128]{0:T(512)(128)(4,1)S(1)}, pred[128]{0:T(512)(128)(4,1)}, u32[]{:S(2)}) copy-start(pred[128]{0:T(512)(128)(4,1)} %get-tuple-element.359) | copy-start | bytes 388
  165.0 117.4 %copy-start.122 = (pred[16]{0:T(512)(128)(4,1)S(1)}, pred[16]{0:T(512)(128)(4,1)}, u32[]{:S(2)}) copy-start(pred[16]{0:T(512)(128)(4,1)} %iota_compare_fusion.2) | copy-start | bytes 52
  317.3 132.9 %all-to-all-start.1 = ((f32[16,1,1280]{2,1,0:T(1,128)}), f32[16,1,1280]{2,1,0:T(1,128)}, u32[]{:S(2)}, u32[]{:S(2)}) async-start(f32[16,1,1280]{2,1,0:T(1,128)} %reshape.1992), calls=%async_computation.1 | async-start | bytes 163840 | tf_op jit(solution)/shard_map/all_to_all | solution.py:137
  322.3 127.0 %collective-permute-start.2 = (f32[64,1,64]{2,0,1:T(8,128)}, f32[64,1,64]{2,0,1:T(8,128)}, u32[]{:S(2)}, u32[]{:S(2)}) collective-permute-start(f32[64,1,64]{2,0,1:T(8,128)} %copy.460), channel_id=1, source_target_pairs={{0,16},{16,32},{32,48},{48,64},{64,80},{80,96},{96,112},{112,128},... | collective-permute-start | bytes 49160 | tf_op jit(solution)/shard_map/ppermute | solution.py:16
  324.8 124.5 %collective-permute-start.3 = (f32[64,1,64]{2,0,1:T(8,128)}, f32[64,1,64]{2,0,1:T(8,128)}, u32[]{:S(2)}, u32[]{:S(2)}) collective-permute-start(f32[64,1,64]{2,0,1:T(8,128)} %copy.461), channel_id=1, source_target_pairs={{16,0},{32,16},{48,32},{64,48},{80,64},{96,80},{112,96},{128,112},... | collective-permute-start | bytes 49160 | tf_op jit(solution)/shard_map/ppermute | solution.py:19
  339.5 108.0 %copy-start.72 = (f32[128]{0:T(128)S(1)}, f32[128]{0:T(128)}, u32[]{:S(2)}) copy-start(f32[128]{0:T(128)} %copy-done.71) | copy-start | bytes 1540
  339.5 110.6 %copy-start.67 = (pred[128]{0:T(512)(128)(4,1)S(1)}, pred[128]{0:T(512)(128)(4,1)}, u32[]{:S(2)}) copy-start(pred[128]{0:T(512)(128)(4,1)} %copy-done.66) | copy-start | bytes 388
  339.6 110.6 %copy-start.84 = (pred[128]{0:T(512)(128)(4,1)S(1)}, pred[128]{0:T(512)(128)(4,1)}, u32[]{:S(2)}) copy-start(pred[128]{0:T(512)(128)(4,1)} %get-tuple-element.361) | copy-start | bytes 388
  339.6 110.6 %copy-start.118 = (pred[128]{0:T(512)(128)(4,1)S(1)}, pred[128]{0:T(512)(128)(4,1)}, u32[]{:S(2)}) copy-start(pred[128]{0:T(512)(128)(4,1)} %get-tuple-element.359) | copy-start | bytes 388
  339.6 112.4 %copy-start.123 = (pred[16]{0:T(512)(128)(4,1)S(1)}, pred[16]{0:T(512)(128)(4,1)}, u32[]{:S(2)}) copy-start(pred[16]{0:T(512)(128)(4,1)} %iota_compare_fusion.2) | copy-start | bytes 52
  342.5 110.2 %copy-start.65 = (pred[320]{0:T(512)(128)(4,1)S(1)}, pred[320]{0:T(512)(128)(4,1)}, u32[]{:S(2)}) copy-start(pred[320]{0:T(512)(128)(4,1)} %get-tuple-element.355) | copy-start | bytes 964
  342.5 110.4 %copy-start.74 = (pred[320]{0:T(512)(128)(4,1)S(1)}, pred[320]{0:T(512)(128)(4,1)}, u32[]{:S(2)}) copy-start(pred[320]{0:T(512)(128)(4,1)} %get-tuple-element.356) | copy-start | bytes 964
  342.5 110.4 %copy-start.112 = (pred[320]{0:T(512)(128)(4,1)S(1)}, pred[320]{0:T(512)(128)(4,1)}, u32[]{:S(2)}) copy-start(pred[320]{0:T(512)(128)(4,1)} %get-tuple-element.354) | copy-start | bytes 964
  (108 other events, 865.2 us)
where the time goes:
time: 570 us; the launch traced here: 567 us
  blocking collectives  410 us (72%)
  local copies, waits for them, and re-layouts  94 us (16%)
  other arithmetic  34.3 us (6%)
  starting transfers between devices  17 us (3%)
  between operations  9.18 us (2%)
    psum x1, blocking collectives, on_device(): coarse_rhs = lax.psum(coarse_partial, ('gx', 'gy'))  109 us
    psum x1, blocking collectives, on_device(): lax.psum((precond_local, curvature_local, norm_local), ('gx', 'gy'))  102 us
    unnamed x1, blocking collectives  99.5 us
    psum x1, blocking collectives, on_device(): fresh_norm = lax.psum(jnp.sum(residual_out * residual_out), ('gx', 'gy'))  99.4 us
    mul x78, local copies, waits for them, and re-layouts, contract(): total = total + matrices[index][:, None, None, :] * moved[index][None]  28.3 us
    unnamed x280, local copies, waits for them, and re-layouts  12 us
    all_to_all x2, starting transfers between devices, face_sum(): lax.all_to_all(outgoing, 'gy', split_axis=1, concat_axis=1, tiled=True)  11.8 us
  transfers between devices with their start and end apart: 6, of which 0 were waited for; matrix products, arithmetic and copies ran while one was open for 12% of the time, Pallas kernels for 0%

commit v1 on v0

--- a/solution.py
+++ b/solution.py
@@ -191,7 +191,7 @@
     coarse_partial = jax.ops.segment_sum(
         corners.reshape(-1), vertex_ids.reshape(-1), num_segments=coarse_inverse.shape[1]
     )
-    coarse_rhs = lax.psum(coarse_partial, ("gx", "gy"))
+    coarse_rhs = lax.psum(lax.psum(coarse_partial, "gy"), "gx")
     own_values = jnp.dot(coarse_inverse, coarse_rhs, precision=top_precision)
     coarse_sol = lax.all_gather(own_values, ("gx", "gy"), axis=0, tiled=True)
     smooth = fdm_solve(rmask.reshape(EDGE, EDGE, EDGE, -1), fdm_vectors, fdm_values).reshape(

time: 570 us -> 632 us (1.11)
  blocking collectives: 410 us -> 472 us
    psum x1 -> x2, blocking collectives: 109 us -> 167 us  [on_device(): coarse_rhs = lax.psum(lax.psum(coarse_partial, 'gy'), 'gx')]
  transfers between devices with their start and end apart: 6 -> 6, of which waited for: 0 -> 0; matrix products, arithmetic and copies ran while one was open for 12% -> 11% of each run, Pallas kernels for 0% -> 0%
where the time goes in v1:
time: 632 us; the launch traced here: 629 us
  blocking collectives  472 us (75%)
  local copies, waits for them, and re-layouts  94.2 us (15%)
  other arithmetic  34.4 us (5%)
  starting transfers between devices  16.5 us (3%)
  between operations  9.01 us (1%)
    psum x2, blocking collectives, on_device(): coarse_rhs = lax.psum(lax.psum(coarse_partial, 'gy'), 'gx')  167 us
    psum x1, blocking collectives, on_device(): lax.psum((precond_local, curvature_local, norm_local), ('gx', 'gy'))  103 us
    unnamed x1, blocking collectives  102 us
    psum x1, blocking collectives, on_device(): fresh_norm = lax.psum(jnp.sum(residual_out * residual_out), ('gx', 'gy'))  99.7 us
    mul x78, local copies, waits for them, and re-layouts, contract(): total = total + matrices[index][:, None, None, :] * moved[index][None]  28.4 us
  transfers between devices with their start and end apart: 6, of which 0 were waited for; matrix products, arithmetic and copies ran while one was open for 11% of the time, Pallas kernels for 0%

profile of v1, /device:TPU:1, one launch (start us, length us, event | category | flops | bytes accessed | tf_op | source)
XLA Modules:
  0.0 629.2 jit_solution(7808026925009426409)
XLA Ops:
  6.8 2.2 copy.389
  9.0 2.5 reshape.1869
  14.5 7.6 %all-to-all-start = ((f32[16,1,1280]{2,1,0:T(1,128)}), f32[16,1,1280]{2,1,0:T(1,128)}, u32[]{:S(2)}, u32[]{:S(2)}) async-start(f32[16,1,1280]{2,1,0:T(1,128)} %reshape.1990), calls=%async_computation | async-start | bytes 163840 | tf_op jit(solution)/shard_map/all_to_all | solution.py:137
  23.6 2.5 collective-permute-start
  30.1 5.9 scatter_custom_fusion.1
  36.0 60.5 %psum.42 = f32[8192]{0:T(1024)S(1)} all-reduce(f32[8192]{0:T(1024)S(1)} %scatter_custom_fusion.1), channel_id=1, replica_groups=mesh['gx'=32,'gy'=16] {'gy'}, use_global_device_ids=true, to_apply=%region_2.5 | all-reduce | flops 8192 | bytes 65536 | tf_op jit(solution)/shard_map/psum | solution.py:194
  96.5 106.5 %psum.43 = f32[8192]{0:T(1024)S(1)} all-reduce(f32[8192]{0:T(1024)S(1)} %psum.42), channel_id=1, replica_groups=mesh['gx'=32,'gy'=16] {'gx'}, use_global_device_ids=true, to_apply=%region_3.6 | all-reduce | flops 8192 | bytes 65536 | tf_op jit(solution)/shard_map/psum | solution.py:194
  228.4 102.5 %all-reduce = f32[8192]{0:T(1024)S(1)} all-reduce(f32[8192]{0:T(1024)S(1)} %dynamic-update-slice.36), channel_id=1, replica_groups=mesh['gx'=32,'gy'=16] {'gx','gy'}, use_global_device_ids=true, to_apply=%add | all-reduce | flops 8192 | bytes 65536
  330.8 10.5 %gather_fusion = f32[1024]{0:T(1024)} fusion(f32[8192]{0:T(1024)S(1)} %all-reduce, s32[1024]{0:T(1024)S(1)} %fusion.40), kind=kCustom, calls=%fused_computation.4 | custom fusion | bytes 12288 | tf_op jit(solution)/shard_map/gather | solution.py:201
  345.1 2.3 scatter_custom_fusion
  347.3 2.6 reshape.1876
  350.0 3.4 fusion.54
  353.4 1.9 copy.456
  363.4 1.9 multiply_reduce_fusion
  371.4 2.2 copy.428
  373.7 2.4 reshape.1886
  379.0 4.1 all-to-all-start.1
  400.8 2.9 add_reduce_fusion
  404.9 103.1 %all-reduce.2 = (f32[]{:T(128)}, f32[]{:T(128)}) all-reduce(f32[]{:T(128)} %get-tuple-element.150, f32[]{:T(128)S(6)} %add.972), channel_id=1, replica_groups=mesh['gx'=32,'gy'=16] {'gx','gy'}, use_global_device_ids=true, to_apply=%region_5.8 | all-reduce | flops 2 | bytes 16 | tf_op jit(solution)/shard_map/psum | solution.py:207
  511.9 1.7 reduce.27
  514.9 2.5 scatter_custom_fusion.2
  517.4 2.6 reshape.1893
  520.0 2.9 fusion.53
  527.2 99.7 %all-reduce.1 = (f32[]{:T(128)}, f32[]{:T(128)}) all-reduce(f32[]{:T(128)} %get-tuple-element.156, f32[]{:T(128)} %get-tuple-element.149), channel_id=1, replica_groups=mesh['gx'=32,'gy'=16] {'gx','gy'}, use_global_device_ids=true, to_apply=%region_12.15 | all-reduce | flops 2 | bytes 16 | tf_op jit(solution)/shard_map/psum | solution.py:212
  (524 shorter events, 83.1 us)
Async XLA Ops:
  0.6 206.0 %copy-start = (f32[16,8192]{1,0:T(8,128)S(1)}, f32[16,8192]{1,0:T(8,128)}, u32[]{:S(2)}) copy-start(f32[16,8192]{1,0:T(8,128)} %param.48) | copy-start | bytes 1572868
  9.0 194.4 %copy-start.2 = (bf16[3,512,128]{2,1,0:T(8,128)(2,1)S(1)}, bf16[3,512,128]{2,1,0:T(8,128)(2,1)}, u32[]{:S(2)}) copy-start(bf16[3,512,128]{2,1,0:T(8,128)(2,1)} %param.44) | copy-start | bytes 1179652
  11.5 192.9 %copy-start.1 = (bf16[3,512,128]{2,1,0:T(8,128)(2,1)S(1)}, bf16[3,512,128]{2,1,0:T(8,128)(2,1)}, u32[]{:S(2)}) copy-start(bf16[3,512,128]{2,1,0:T(8,128)(2,1)} %param.43) | copy-start | bytes 1179652
  12.5 192.9 %copy-start.110 = (s32[1024]{0:T(1024)}, s32[1024]{0:T(1024)S(1)}, u32[]{:S(2)}) copy-start(s32[1024]{0:T(1024)S(1)} %get-tuple-element.373) | copy-start | bytes 12292
  14.5 327.0 %all-to-all-start = ((f32[16,1,1280]{2,1,0:T(1,128)}), f32[16,1,1280]{2,1,0:T(1,128)}, u32[]{:S(2)}, u32[]{:S(2)}) async-start(f32[16,1,1280]{2,1,0:T(1,128)} %reshape.1990), calls=%async_computation | async-start | bytes 163840 | tf_op jit(solution)/shard_map/all_to_all | solution.py:137
  23.4 318.0 %copy-start.66 = (pred[128]{0:T(512)(128)(4,1)}, pred[128]{0:T(512)(128)(4,1)S(1)}, u32[]{:S(2)}) copy-start(pred[128]{0:T(512)(128)(4,1)S(1)} %get-tuple-element.360) | copy-start | bytes 388
  23.6 317.7 %collective-permute-start = (f32[64,1,64]{2,0,1:T(8,128)S(1)}, f32[64,1,64]{2,0,1:T(8,128)S(1)}, u32[]{:S(2)}, u32[]{:S(2)}) collective-permute-start(f32[64,1,64]{2,0,1:T(8,128)S(1)} %copy.454), channel_id=1, source_target_pairs={{0,16},{16,32},{32,48},{48,64},{64,80},{80,96},{96,112},{112,128},... | collective-permute-start | bytes 49160 | tf_op jit(solution)/shard_map/ppermute | solution.py:16
  26.8 314.5 %collective-permute-start.1 = (f32[64,1,64]{2,0,1:T(8,128)}, f32[64,1,64]{2,0,1:T(8,128)S(1)}, u32[]{:S(2)}, u32[]{:S(2)}) collective-permute-start(f32[64,1,64]{2,0,1:T(8,128)} %copy.455), channel_id=1, source_target_pairs={{16,0},{32,16},{48,32},{64,48},{80,64},{96,80},{112,96},{128,112},... | collective-permute-start | bytes 49160 | tf_op jit(solution)/shard_map/ppermute | solution.py:19
  203.4 23.4 %copy-start.46 = (f32[8]{0:T(128)}, f32[8]{0:T(128)S(1)}, u32[]{:S(2)}) copy-start(f32[8]{0:T(128)S(1)} %get-tuple-element.348) | copy-start | bytes 100
  203.4 24.1 %copy-start.44 = (f32[8]{0:T(128)}, f32[8]{0:T(128)S(1)}, u32[]{:S(2)}) copy-start(f32[8]{0:T(128)S(1)} %get-tuple-element.347) | copy-start | bytes 100
  210.9 130.5 %copy-start.83 = (pred[128]{0:T(512)(128)(4,1)S(1)}, pred[128]{0:T(512)(128)(4,1)}, u32[]{:S(2)}) copy-start(pred[128]{0:T(512)(128)(4,1)} %get-tuple-element.361) | copy-start | bytes 388
  210.9 130.5 %copy-start.117 = (pred[128]{0:T(512)(128)(4,1)S(1)}, pred[128]{0:T(512)(128)(4,1)}, u32[]{:S(2)}) copy-start(pred[128]{0:T(512)(128)(4,1)} %get-tuple-element.359) | copy-start | bytes 388
  223.4 120.5 %copy-start.122 = (pred[16]{0:T(512)(128)(4,1)S(1)}, pred[16]{0:T(512)(128)(4,1)}, u32[]{:S(2)}) copy-start(pred[16]{0:T(512)(128)(4,1)} %iota_compare_fusion.2) | copy-start | bytes 52
  379.0 132.9 %all-to-all-start.1 = ((f32[16,1,1280]{2,1,0:T(1,128)}), f32[16,1,1280]{2,1,0:T(1,128)}, u32[]{:S(2)}, u32[]{:S(2)}) async-start(f32[16,1,1280]{2,1,0:T(1,128)} %reshape.1992), calls=%async_computation.1 | async-start | bytes 163840 | tf_op jit(solution)/shard_map/all_to_all | solution.py:137
  383.9 127.0 %collective-permute-start.2 = (f32[64,1,64]{2,0,1:T(8,128)}, f32[64,1,64]{2,0,1:T(8,128)}, u32[]{:S(2)}, u32[]{:S(2)}) collective-permute-start(f32[64,1,64]{2,0,1:T(8,128)} %copy.460), channel_id=1, source_target_pairs={{0,16},{16,32},{32,48},{48,64},{64,80},{80,96},{96,112},{112,128},... | collective-permute-start | bytes 49160 | tf_op jit(solution)/shard_map/ppermute | solution.py:16
  386.0 125.0 %collective-permute-start.3 = (f32[64,1,64]{2,0,1:T(8,128)}, f32[64,1,64]{2,0,1:T(8,128)}, u32[]{:S(2)}, u32[]{:S(2)}) collective-permute-start(f32[64,1,64]{2,0,1:T(8,128)} %copy.461), channel_id=1, source_target_pairs={{16,0},{32,16},{48,32},{64,48},{80,64},{96,80},{112,96},{128,112},... | collective-permute-start | bytes 49160 | tf_op jit(solution)/shard_map/ppermute | solution.py:19
  400.7 108.6 %copy-start.72 = (f32[128]{0:T(128)S(1)}, f32[128]{0:T(128)}, u32[]{:S(2)}) copy-start(f32[128]{0:T(128)} %copy-done.71) | copy-start | bytes 1540
  400.7 111.1 %copy-start.67 = (pred[128]{0:T(512)(128)(4,1)S(1)}, pred[128]{0:T(512)(128)(4,1)}, u32[]{:S(2)}) copy-start(pred[128]{0:T(512)(128)(4,1)} %copy-done.66) | copy-start | bytes 388
  400.7 111.1 %copy-start.84 = (pred[128]{0:T(512)(128)(4,1)S(1)}, pred[128]{0:T(512)(128)(4,1)}, u32[]{:S(2)}) copy-start(pred[128]{0:T(512)(128)(4,1)} %get-tuple-element.361) | copy-start | bytes 388
  400.7 111.1 %copy-start.118 = (pred[128]{0:T(512)(128)(4,1)S(1)}, pred[128]{0:T(512)(128)(4,1)}, u32[]{:S(2)}) copy-start(pred[128]{0:T(512)(128)(4,1)} %get-tuple-element.359) | copy-start | bytes 388
  400.8 113.0 %copy-start.123 = (pred[16]{0:T(512)(128)(4,1)S(1)}, pred[16]{0:T(512)(128)(4,1)}, u32[]{:S(2)}) copy-start(pred[16]{0:T(512)(128)(4,1)} %iota_compare_fusion.2) | copy-start | bytes 52
  403.6 110.8 %copy-start.65 = (pred[320]{0:T(512)(128)(4,1)S(1)}, pred[320]{0:T(512)(128)(4,1)}, u32[]{:S(2)}) copy-start(pred[320]{0:T(512)(128)(4,1)} %get-tuple-element.355) | copy-start | bytes 964
  403.6 111.0 %copy-start.74 = (pred[320]{0:T(512)(128)(4,1)S(1)}, pred[320]{0:T(512)(128)(4,1)}, u32[]{:S(2)}) copy-start(pred[320]{0:T(512)(128)(4,1)} %get-tuple-element.356) | copy-start | bytes 964
  403.6 111.0 %copy-start.112 = (pred[320]{0:T(512)(128)(4,1)S(1)}, pred[320]{0:T(512)(128)(4,1)}, u32[]{:S(2)}) copy-start(pred[320]{0:T(512)(128)(4,1)} %get-tuple-element.354) | copy-start | bytes 964
  (108 other events, 867.4 us)
